TPU v7x, 256 devices: a whole 4x4x8 slice. The times are simulated.
256 devices in a mesh: leaf: 32 (over z, y), front: 8 (over x, core).
Axes of the slice: x: 4, y: 4, z: 8, core: 2. Of those that a mesh axis runs over, the one named last changes fastest.
Arguments:
- front: float32 [40960, 8192], P('leaf', 'front'), may hold values from -2.5 to 515.06
- child_blocks: float32 [32, 32, 128, 1024], P('leaf', None, None, 'front'), may hold values from -0.1 to 0.25
- child_map: int32 [32, 32, 8], P('leaf', None, 'front'), may hold values from 0 to 79, as said below
- pattern: int32 [320, 64], P('leaf', 'front'), may hold values 0 or 1
Outputs:
- factored: float32 [40960, 8192], P('leaf', 'front')
Inputs may be any that keep to these rules, and one draw needn't show every extreme that they name: `child_map`: for one receiving leaf index and one front index, the contribution blocks of the different senders name different blocks, and every block on the front's diagonal among the receiver's blocks is named by one of them.
All inputs are finite; a program needn't handle non-finite values. No bound on the sum of `pattern` on one device may be relied on, other than what follows from the above.
Results may differ from a plain program's by a relative error of at most 0.0003.
Values sent between devices are 32-bit elements; how exact they have to be, the bound alone decides.
A program may use at most 128 MiB of HBM per device.

v0:
```python
import jax
import jax.numpy as jnp
from jax import lax
from jax.sharding import PartitionSpec as P

PANELS = 4


def from_root(value, axis, root):
    mine = lax.axis_index(axis) == root
    return lax.psum(jnp.where(mine, value, jnp.zeros_like(value)), axis)


def form_column(column, inverse, factor, row_block, panel, row_count):
    solved = jnp.dot(column, inverse.T, precision=lax.Precision.HIGHEST)
    lower = jnp.where(row_block[:, None] > panel, solved, 0.0)
    return jnp.where(row_block[:, None] == panel, jnp.tile(factor, (row_count, 1)), lower)


def apply_update(matrix_part, lower, across_part, col_part, row_block, panel):
    product = jnp.dot(lower, across_part.T, precision=lax.Precision.HIGHEST)
    active = (row_block[:, None] >= col_part[None, :]) & (col_part[None, :] > panel)
    return jnp.where(active, matrix_part - product, matrix_part)


def body(front, child_blocks, child_map, pattern):
    highest = lax.Precision.HIGHEST
    block_size = child_blocks.shape[2]
    row_count = pattern.shape[0]
    col_count = pattern.shape[1]
    leaf_count = lax.axis_size("leaf")
    leaf_at = lax.axis_index("leaf")
    front_at = lax.axis_index("front")
    arrived, arrived_map = (
        lax.all_to_all(child_blocks, "leaf", split_axis=1, concat_axis=0, tiled=True),
        lax.all_to_all(
            child_map.astype(jnp.float32), "leaf", split_axis=1, concat_axis=0, tiled=True
        ),
    )
    targets = arrived_map.reshape(-1).astype(jnp.int32)
    slots = jnp.arange(row_count * col_count, dtype=jnp.int32)
    selector = (slots[:, None] == targets[None, :]).astype(jnp.float32)
    summed = jnp.dot(
        selector, arrived.reshape(leaf_count, block_size * block_size), precision=highest
    )
    added = (
        summed.reshape(row_count, col_count, block_size, block_size)
        .transpose(0, 2, 1, 3)
        .reshape(front.shape)
    )
    global_rows = leaf_at * row_count + jnp.arange(row_count, dtype=jnp.int32)
    global_cols = front_at * col_count + jnp.arange(col_count, dtype=jnp.int32)
    keep = ((pattern == 1) | (global_rows[:, None] == global_cols[None, :])) & (
        global_rows[:, None] >= global_cols[None, :]
    )
    matrix = jnp.where(
        keep[:, None, :, None],
        (front + added).reshape(row_count, block_size, col_count, block_size),
        0.0,
    ).reshape(front.shape)
    row_block = jnp.repeat(global_rows, block_size)
    col_block = jnp.repeat(global_cols, block_size)
    identity = jnp.eye(block_size, dtype=jnp.float32)
    for panel in range(PANELS):
        pivot_leaf = panel // row_count
        pivot_front = panel // col_count
        local_row = panel % row_count * block_size
        local_col = panel % col_count * block_size
        is_owner = (leaf_at == pivot_leaf) & (front_at == pivot_front)
        pivot = matrix[local_row : local_row + block_size, local_col : local_col + block_size]
        symmetric = jnp.tril(pivot) + jnp.tril(pivot, -1).T
        factor = jnp.linalg.cholesky(jnp.where(is_owner, symmetric, identity))
        inverse = lax.linalg.triangular_solve(factor, identity, left_side=True, lower=True)
        column = matrix[:, local_col : local_col + block_size]
        inverse = from_root(inverse, "leaf", pivot_leaf)
        lower = form_column(column, inverse, factor, row_block, panel, row_count)
        lower = from_root(lower, "front", pivot_front)
        chooser = (global_cols[:, None] == global_rows[None, :]).astype(jnp.float32)
        matched = jnp.dot(
            chooser, lower.reshape(row_count, block_size * block_size), precision=highest
        )
        across = lax.psum(matched, "leaf").reshape(col_count * block_size, block_size)
        matrix = apply_update(matrix, lower, across, col_block, row_block, panel)
        current = matrix[:, local_col : local_col + block_size]
        matrix = matrix.at[:, local_col : local_col + block_size].set(
            jnp.where(front_at == pivot_front, lower, current)
        )
    return matrix


def solution(mesh):
    placed = (
        P("leaf", "front"),
        P("leaf", None, None, "front"),
        P("leaf", None, "front"),
        P("leaf", "front"),
    )
    return jax.shard_map(
        body, mesh=mesh, in_specs=placed, out_specs=P("leaf", "front"), check_vma=False
    )
```

profile of v0, /device:TPU:167, one launch (start us, length us, event | category | flops | bytes accessed | tf_op | source)
XLA Modules:
  0.0 1666.7 jit_solution(10896939773123481023)
XLA Ops:
  7.3 13.5 all_to_all.8
  20.8 7.9 all-to-all-start.1
  30.5 42.0 %all-to-all-done.1 = f32[1,32,128,128]{3,2,0,1:T(8,128)S(1)} async-done(((f32[1,32,128,128]{3,2,0,1:T(8,128)}), f32[1,32,128,128]{3,2,0,1:T(8,128)S(1)}, u32[]{:S(2)}, u32[]{:S(2)}) %all-to-all-start.1) | async-done | bytes 2097184 | tf_op jit(solution)/shard_map/all_to_all | solution.py:35
  72.4 3.6 fusion.9
  76.4 4.7 fusion
  81.1 2.3 copy-done.2
  84.7 11.7 cholesky.74
  97.8 10.1 custom-call.8
  109.0 137.2 %all-reduce.13.cloned.1.call-done = f32[128,128]{1,0:T(8,128)} async-done(((f32[128,128]{1,0:T(8,128)}), f32[128,128]{1,0:T(8,128)}) %all-reduce.13.cloned.1.call-update) | async-done | bytes 65552 | tf_op jit(solution)/shard_map/psum | solution.py:11
  246.3 2.7 fusion.2
  249.0 69.8 %all-reduce.15.cloned.1.call-done = f32[1280,128]{1,0:T(8,128)} async-done(((f32[1280,128]{1,0:T(8,128)}), f32[1280,128]{1,0:T(8,128)}) %all-reduce.15.cloned.1.call-update) | async-done | bytes 655376 | tf_op jit(solution)/shard_map/psum | solution.py:11
  318.8 1.3 reshape.295
  322.4 140.6 %all-reduce.17.cloned.1.call-done = f32[1024,128]{1,0:T(8,128)} async-done(((f32[1024,128]{1,0:T(8,128)}), f32[1024,128]{1,0:T(8,128)}) %all-reduce.17.cloned.1.call-update) | async-done | bytes 524304 | tf_op jit(solution)/shard_map/psum | solution.py:82
  463.0 7.1 subtract_select_fusion.3
  471.0 2.3 copy-done.1
  474.5 11.7 cholesky.85
  487.7 9.8 custom-call.9
  498.6 137.0 %all-reduce.19.cloned.1.call-done = f32[128,128]{1,0:T(8,128)} async-done(((f32[128,128]{1,0:T(8,128)}), f32[128,128]{1,0:T(8,128)}) %all-reduce.19.cloned.1.call-update) | async-done | bytes 65552 | tf_op jit(solution)/shard_map/psum | solution.py:11
  635.7 2.7 fusion.4
  638.4 69.8 %all-reduce.21.cloned.1.call-done = f32[1280,128]{1,0:T(8,128)} async-done(((f32[1280,128]{1,0:T(8,128)}), f32[1280,128]{1,0:T(8,128)}) %all-reduce.21.cloned.1.call-update) | async-done | bytes 655376 | tf_op jit(solution)/shard_map/psum | solution.py:11
  711.6 141.1 %all-reduce.23.cloned.1.call-done = f32[1024,128]{1,0:T(8,128)} async-done(((f32[1024,128]{1,0:T(8,128)}), f32[1024,128]{1,0:T(8,128)}) %all-reduce.23.cloned.1.call-update) | async-done | bytes 524304 | tf_op jit(solution)/shard_map/psum | solution.py:82
  852.7 8.5 subtract_select_fusion.2
  861.2 5.9 copy.123
  867.1 1.8 select_select_fusion.2
  872.1 11.7 cholesky.96
  885.1 9.8 custom-call.10
  896.4 136.5 %all-reduce.25.cloned.1.call-done = f32[128,128]{1,0:T(8,128)} async-done(((f32[128,128]{1,0:T(8,128)}), f32[128,128]{1,0:T(8,128)}) %all-reduce.25.cloned.1.call-update) | async-done | bytes 65552 | tf_op jit(solution)/shard_map/psum | solution.py:11
  1032.9 2.6 fusion.6
  1035.6 69.8 %all-reduce.27.cloned.1.call-done = f32[1280,128]{0,1:T(8,128)} async-done(((f32[1280,128]{0,1:T(8,128)}), f32[1280,128]{0,1:T(8,128)}) %all-reduce.27.cloned.1.call-update) | async-done | bytes 655376 | tf_op jit(solution)/shard_map/psum | solution.py:11
  1105.4 1.3 copy.131
  1108.3 1.8 compare_and_fusion.2
  1110.1 1.4 copy.133
  1112.1 137.5 %all-reduce.29.cloned.1.call-done = f32[1024,128]{1,0:T(8,128)} async-done(((f32[1024,128]{1,0:T(8,128)}), f32[1024,128]{1,0:T(8,128)}) %all-reduce.29.cloned.1.call-update) | async-done | bytes 524304 | tf_op jit(solution)/shard_map/psum | solution.py:82
  1249.6 7.5 subtract_select_fusion.1
  1257.9 2.3 copy-done
  1261.4 11.7 cholesky.107
  1274.6 9.8 custom-call.11
  1285.9 136.5 %all-reduce.31.cloned.1.call-done = f32[128,128]{1,0:T(8,128)} async-done(((f32[128,128]{1,0:T(8,128)}), f32[128,128]{1,0:T(8,128)}) %all-reduce.31.cloned.1.call-update) | async-done | bytes 65552 | tf_op jit(solution)/shard_map/psum | solution.py:11
  1422.4 2.7 fusion.8
  1425.1 69.8 %all-reduce.33.cloned.1.call-done = f32[1280,128]{0,1:T(8,128)} async-done(((f32[1280,128]{0,1:T(8,128)}), f32[1280,128]{0,1:T(8,128)}) %all-reduce.33.cloned.1.call-update) | async-done | bytes 655376 | tf_op jit(solution)/shard_map/psum | solution.py:11
  1494.9 2.2 copy.141
  1498.4 1.3 fusion.34
  1499.7 1.9 reshape.302
  1501.7 1.4 copy.143
  1503.8 138.8 %all-reduce.35.cloned.1.call-done = f32[1024,128]{1,0:T(8,128)} async-done(((f32[1024,128]{1,0:T(8,128)}), f32[1024,128]{1,0:T(8,128)}) %all-reduce.35.cloned.1.call-update) | async-done | bytes 524304 | tf_op jit(solution)/shard_map/psum | solution.py:82
  1642.6 8.3 subtract_select_fusion
  1650.9 2.7 fusion.13
  1653.6 5.9 copy.145
  (110 shorter events, 31.9 us)
Async XLA Ops:
  20.8 51.6 %all-to-all-start.1 = ((f32[1,32,128,128]{3,2,0,1:T(8,128)}), f32[1,32,128,128]{3,2,0,1:T(8,128)S(1)}, u32[]{:S(2)}, u32[]{:S(2)}) async-start(f32[1,32,128,128]{3,2,0,1:T(8,128)} %bitcast.130), calls=%async_computation.1 | async-start | bytes 4194304 | tf_op jit(solution)/shard_map/all_to_all | solution.py:35
  28.7 217.6 %all-reduce.13.cloned.1.call-start = ((), (), s32[]{:S(2)}) async-start(), calls=%async_computation.2 | async-start | bytes 131072 | tf_op jit(solution)/shard_map/psum | solution.py:11
  81.1 2.4 copy-start.2
  108.9 209.9 %all-reduce.15.cloned.1.call-start = ((), (), s32[]{:S(2)}) async-start(), calls=%async_computation.3 | async-start | bytes 1310720 | tf_op jit(solution)/shard_map/psum | solution.py:11
  249.0 214.0 %all-reduce.17.cloned.1.call-start = ((), (), s32[]{:S(2)}) async-start(), calls=%async_computation.4 | async-start | bytes 1048576 | tf_op jit(solution)/shard_map/psum | solution.py:82
  318.8 144.2 %copy-start.4 = (f32[1280,128]{1,0:T(8,128)S(1)}, f32[1280,128]{1,0:T(8,128)}, u32[]{:S(2)}) copy-start(f32[1280,128]{1,0:T(8,128)} %all-reduce.15.cloned.1.call-done) | copy-start | bytes 1966084
  321.5 314.2 %all-reduce.19.cloned.1.call-start = ((), (), s32[]{:S(2)}) async-start(), calls=%async_computation.5 | async-start | bytes 131072 | tf_op jit(solution)/shard_map/psum | solution.py:11
  471.0 2.4 copy-start.1
  498.4 209.8 %all-reduce.21.cloned.1.call-start = ((), (), s32[]{:S(2)}) async-start(), calls=%async_computation.6 | async-start | bytes 1310720 | tf_op jit(solution)/shard_map/psum | solution.py:11
  638.4 214.3 %all-reduce.23.cloned.1.call-start = ((), (), s32[]{:S(2)}) async-start(), calls=%async_computation.7 | async-start | bytes 1048576 | tf_op jit(solution)/shard_map/psum | solution.py:82
  708.2 144.5 %copy-start.6 = (f32[1280,128]{1,0:T(8,128)S(1)}, f32[1280,128]{1,0:T(8,128)}, u32[]{:S(2)}) copy-start(f32[1280,128]{1,0:T(8,128)} %all-reduce.21.cloned.1.call-done) | copy-start | bytes 1966084
  710.9 322.0 %all-reduce.25.cloned.1.call-start = ((), (), s32[]{:S(2)}) async-start(), calls=%async_computation.8 | async-start | bytes 131072 | tf_op jit(solution)/shard_map/psum | solution.py:11
  895.9 209.6 %all-reduce.27.cloned.1.call-start = ((), (), s32[]{:S(2)}) async-start(), calls=%async_computation.9 | async-start | bytes 1310720 | tf_op jit(solution)/shard_map/psum | solution.py:11
  1035.6 214.0 %all-reduce.29.cloned.1.call-start = ((), (), s32[]{:S(2)}) async-start(), calls=%async_computation.10 | async-start | bytes 1048576 | tf_op jit(solution)/shard_map/psum | solution.py:82
  1106.7 142.9 %copy-start.3 = (f32[1280,128]{0,1:T(8,128)S(1)}, f32[1280,128]{0,1:T(8,128)}, u32[]{:S(2)}) copy-start(f32[1280,128]{0,1:T(8,128)} %all-reduce.27.cloned.1.call-done) | copy-start | bytes 1966084
  1108.3 314.1 %all-reduce.31.cloned.1.call-start = ((), (), s32[]{:S(2)}) async-start(), calls=%async_computation.11 | async-start | bytes 131072 | tf_op jit(solution)/shard_map/psum | solution.py:11
  1257.9 2.4 copy-start
  1285.3 209.6 %all-reduce.33.cloned.1.call-start = ((), (), s32[]{:S(2)}) async-start(), calls=%async_computation.12 | async-start | bytes 1310720 | tf_op jit(solution)/shard_map/psum | solution.py:11
  1425.1 217.5 %all-reduce.35.cloned.1.call-start = ((), (), s32[]{:S(2)}) async-start(), calls=%async_computation.13 | async-start | bytes 1048576 | tf_op jit(solution)/shard_map/psum | solution.py:82
  1494.9 147.7 %copy-start.5 = (f32[1280,128]{0,1:T(8,128)S(1)}, f32[1280,128]{0,1:T(8,128)}, u32[]{:S(2)}) copy-start(f32[1280,128]{0,1:T(8,128)} %all-reduce.33.cloned.1.call-done) | copy-start | bytes 1966084
Sparse Core Ops, SparseCore 0:
  109.0 137.1 all-reduce.12
  249.1 69.6 all-reduce.14
  322.2 140.7 all-reduce.16
  498.5 137.0 all-reduce.18
  638.5 69.6 all-reduce.20
  711.8 140.7 all-reduce.22
  896.0 136.8 all-reduce.24
  1035.7 69.6 all-reduce.26
  1108.8 140.7 all-reduce.28
  1285.4 136.9 all-reduce.30
  1425.2 69.6 all-reduce.32
  1501.8 140.7 all-reduce.34
where the time goes:
time: 1690 us; the launch traced here: 1670 us
  waiting for transfers between devices  1430 us (85%)
  other arithmetic  113 us (7%)
  matrix products  52.1 us (3%)
  local copies, waits for them, and re-layouts  37.9 us (2%)
    psum x8, waiting for transfers between devices, from_root(): return lax.psum(jnp.where(mine, value, jnp.zeros_like(value)), axis)  826 us
    psum x4, waiting for transfers between devices, body(): lax.psum(matched, 'leaf').reshape(col_count * block_size, block_size)  558 us
    another operation x12, other arithmetic, body(): factor = jnp.linalg.cholesky(jnp.where(is_owner, symmetric, identity))  49.8 us
    another operation x8, other arithmetic, body(): lax.linalg.triangular_solve(factor, identity, left_side=True, lower=True)  42.3 us
    all_to_all x1, waiting for transfers between devices, body(): lax.all_to_all(child_blocks, 'leaf', split_axis=1, concat_axis=0, tiled=T...  42 us
  transfers between devices with their start and end apart: 13, of which 13 were waited for; matrix products, arithmetic and copies ran while one was open for 1% of the time, Pallas kernels for 0%

commit v1 on v0

v1 whole, which is shorter than its diff:
```python
import functools

import jax
import jax.numpy as jnp
from jax import lax
from jax.experimental import pallas as pl
from jax.experimental.pallas import tpu as pltpu
from jax.sharding import PartitionSpec as P

B = 128
RB = 10
CB = 8
PANELS = 4
W = PANELS * B
NL = 32
NF = 8
NY = 4
NZ = 8
PIECE = B // NY
NR = CB + PANELS
F32 = jnp.float32
BF16 = jnp.bfloat16
MESH = pl.DeviceIdType.MESH
HBM = pl.BlockSpec(memory_space=pl.ANY)
SMEM = pl.BlockSpec(memory_space=pltpu.SMEM)
VMEM = pl.BlockSpec(memory_space=pltpu.VMEM)


def exchange(
    child, maptile, front, pattern,
    arrived, code, rows, match,
    child_v, front_v, rows_v, map_v, code_v, code_s,
    a_send, a_recv, m_send, m_recv, x_send, x_recv, q_recv, qz_send, qy_send, qa_send, local,
):
    d = lax.axis_index("leaf")
    f = lax.axis_index("front")
    z, y = d // NY, d % NY
    x, core = f // 2, f % 2

    barrier = pltpu.get_barrier_semaphore()

    def greet_leaf(k, _):
        pl.semaphore_signal(
            barrier, inc=1, device_id=(lax.rem(d + k, NL), f), device_id_type=MESH
        )
        return 0

    def greet_front(k, _):
        pl.semaphore_signal(
            barrier, inc=1, device_id=(d, lax.rem(f + k, NF)), device_id_type=MESH
        )
        return 0

    lax.fori_loop(1, NL, greet_leaf, 0)
    lax.fori_loop(1, NF, greet_front, 0)
    pl.semaphore_wait(barrier, NL - 1 + NF - 1)

    def block_copy(k):
        to = lax.rem(d + k, NL)
        return pltpu.make_async_remote_copy(
            src_ref=child.at[to], dst_ref=arrived.at[d], send_sem=a_send.at[k],
            recv_sem=a_recv.at[k], device_id=(to, f), device_id_type=MESH,
        )

    def map_copy(k):
        to = lax.rem(d + k, NL)
        return pltpu.make_async_remote_copy(
            src_ref=maptile.at[to], dst_ref=map_v.at[d], send_sem=m_send.at[k],
            recv_sem=m_recv.at[k], device_id=(to, f), device_id_type=MESH,
        )

    def block_in(k):
        frm = lax.rem(d - k + NL, NL)
        return pltpu.make_async_remote_copy(
            src_ref=child.at[frm], dst_ref=arrived.at[frm], send_sem=a_send.at[k],
            recv_sem=a_recv.at[k], device_id=(frm, f), device_id_type=MESH,
        )

    def map_in(k):
        frm = lax.rem(d - k + NL, NL)
        return pltpu.make_async_remote_copy(
            src_ref=maptile.at[frm], dst_ref=map_v.at[frm], send_sem=m_send.at[k],
            recv_sem=m_recv.at[k], device_id=(frm, f), device_id_type=MESH,
        )

    own_block = pltpu.make_async_copy(child.at[d], arrived.at[d], local.at[0])
    own_map = pltpu.make_async_copy(maptile.at[d], map_v.at[d], local.at[1])

    def send_blocks():
        def step(k, _):
            map_copy(k).start()
            block_copy(k).start()
            return 0

        lax.fori_loop(1, NL, step, 0)

    def receive_blocks():
        def step(k, _):
            map_in(k).wait_recv()
            block_in(k).wait_recv()
            return 0

        lax.fori_loop(1, NL, step, 0)
        own_block.wait()
        own_map.wait()
        lane = lax.broadcasted_iota(jnp.int32, (8, B), 1)

        def latest(s, total):
            return jnp.maximum(total, jnp.where(map_v[s] == lane, s + 1, 0))

        code_v[...] = lax.fori_loop(0, NL, latest, jnp.zeros((8, B), jnp.int32))
        pltpu.make_async_copy(code_v, code, local.at[2]).start()
        pltpu.make_async_copy(code_v, code, local.at[2]).wait()

    own_block.start()
    own_map.start()

    @pl.when(f != 1)
    def _():
        send_blocks()

    def chain_copy(r, to):
        return pltpu.make_async_remote_copy(
            src_ref=rows.at[r], dst_ref=rows.at[r], send_sem=x_send.at[r, 0],
            recv_sem=x_recv.at[r], device_id=(d, to), device_id_type=MESH,
        )

    def pair_copy(r, to):
        return pltpu.make_async_remote_copy(
            src_ref=rows.at[r], dst_ref=rows.at[r], send_sem=x_send.at[r, 1],
            recv_sem=x_recv.at[r], device_id=(d, to), device_id_type=MESH,
        )

    def root_copy(r, to, way):
        return pltpu.make_async_remote_copy(
            src_ref=rows_v.at[r], dst_ref=rows.at[r], send_sem=x_send.at[r, way],
            recv_sem=x_recv.at[r], device_id=(d, to), device_id_type=MESH,
        )

    def root_next(r):
        return jnp.where(r % 2 == 0, 2, NF - 1)

    @pl.when(f == 0)
    def _():
        front_in = pltpu.make_async_copy(front.at[:, pl.ds(0, W)], front_v, local.at[3])
        front_in.start()
        receive_blocks()
        to_vmem = pltpu.make_async_copy(arrived, child_v, local.at[4])
        to_vmem.start()
        to_smem = pltpu.make_async_copy(code_v, code_s, local.at[5])
        to_smem.start()
        front_in.wait()
        to_smem.wait()
        to_vmem.wait()

        def form(r, _):
            r_glob = d * RB + r
            for c in range(PANELS):
                t = code_s[0, r * CB + c]
                block = child_v[jnp.maximum(t - 1, 0)]
                has = (t > 0).astype(F32)
                keep = ((pattern[r, c] == 1) | (r_glob == c)) & (r_glob >= c)
                raw = front_v[pl.ds(r * B, B), c * B : (c + 1) * B]
                rows_v[r, :, c * B : (c + 1) * B] = (raw + block * has) * keep.astype(F32)
            root_copy(r, root_next(r), 0).start()
            root_copy(r, 1, 1).start()
            pltpu.make_async_copy(rows_v.at[r], rows.at[r], local.at[6 + r]).start()
            return 0

        lax.fori_loop(0, RB, form, 0)

        def settle(r, _):
            pltpu.make_async_copy(rows_v.at[r], rows.at[r], local.at[6 + r]).wait()
            return 0

        lax.fori_loop(0, RB, settle, 0)

    pair = f + 1 - 2 * core
    onward = f + 2 - 4 * core
    has_onward = ((core == 0) & (x < 3)) | ((core == 1) & (x > 1))

    @pl.when(f != 0)
    def _():
        def step(r, _):
            pltpu.make_async_remote_copy(
                src_ref=rows.at[r], dst_ref=rows.at[r], send_sem=x_send.at[r, 0],
                recv_sem=x_recv.at[r], device_id=(d, 0), device_id_type=MESH,
            ).wait_recv()

            @pl.when((f >= 2) & (core == r % 2))
            def _():
                @pl.when(has_onward)
                def _():
                    chain_copy(r, onward).start()

                pair_copy(r, pair).start()

            return 0

        lax.fori_loop(0, RB, step, 0)

    @pl.when(f == 1)
    def _():
        send_blocks()

    def where_from(i):
        r = jnp.where(i < CB, f * CB + i, i - CB)
        source = r // RB
        zs, ys = source // NY, source % NY
        return r % RB, ys, lax.rem(z - zs + NZ, NZ)

    def piece_of(ref, i, q):
        return ref.at[i, pl.ds(pl.multiple_of(q * PIECE, PIECE), PIECE)]

    def piece_copy(src, i, q, to_z, to_y, sem):
        return pltpu.make_async_remote_copy(
            src_ref=src, dst_ref=piece_of(match, i, q), send_sem=sem,
            recv_sem=q_recv.at[i, q], device_id=(to_z * NY + to_y, f), device_id_type=MESH,
        )

    def z_copy(src, i, up):
        to = lax.rem(z + (1 if up else NZ - 1), NZ)
        return piece_copy(src, i, y, to, y, qz_send.at[i, 0 if up else 1])

    def match_row(i, act):
        r_loc, ys, zr = where_from(i)
        at_source = (zr == 0) & (y == ys)

        @pl.when(at_source)
        def _():
            whole = pltpu.make_async_copy(rows.at[r_loc], match.at[i], local.at[16 + i])
            mine = piece_of(rows, r_loc, y)
            act(z_copy(mine, i, True))
            act(z_copy(mine, i, False))
            for k in range(1, NY):
                q = lax.rem(y + k, NY)
                act(piece_copy(piece_of(rows, r_loc, q), i, q, z, q, qa_send.at[i, k]))
            for k in range(1, NY):
                q = lax.rem(y + k, NY)
                act(piece_copy(mine, i, y, z, q, qy_send.at[i, k]))
            act(whole, here=True)

        @pl.when(jnp.logical_not(at_source))
        def _():
            mine = piece_of(match, i, y)
            act(None, i, y)

            @pl.when(zr < NZ // 2)
            def _():
                act(z_copy(mine, i, True))

            @pl.when((zr == 0) | (zr > NZ // 2 + 1))
            def _():
                act(z_copy(mine, i, False))

            for k in range(1, NY):
                q = lax.rem(y + k, NY)

                @pl.when((zr != 0) | (q != ys))
                def _():
                    act(piece_copy(mine, i, y, z, q, qy_send.at[i, k]))

                act(None, i, q, late=True)

    def piece_in(i, q):
        piece_copy(piece_of(match, i, q), i, q, z, lax.rem(y + 1, NY), qy_send.at[i, 1]).wait_recv()

    def begin(copy, i=None, q=None, late=False, here=False):
        if copy is not None:
            copy.start()
        elif not late:
            piece_in(i, q)

    def finish(copy, i=None, q=None, late=False, here=False):
        if copy is None:
            if late:
                piece_in(i, q)
        elif here:
            copy.wait()
        else:
            copy.wait_send()

    def run(act):
        def step(n, _):
            match_row(lax.rem(n + CB, NR), act)
            return 0

        lax.fori_loop(0, NR, step, 0)

    run(begin)

    @pl.when(f != 0)
    def _():
        receive_blocks()

    run(finish)

    def sent(k, _):
        map_copy(k).wait_send()
        block_copy(k).wait_send()
        return 0

    lax.fori_loop(1, NL, sent, 0)

    def row_sent(r, _):
        @pl.when(f == 0)
        def _():
            root_copy(r, root_next(r), 0).wait_send()
            root_copy(r, 1, 1).wait_send()

        @pl.when((f >= 2) & (core == r % 2))
        def _():
            @pl.when(has_onward)
            def _():
                chain_copy(r, onward).wait_send()

            pair_copy(r, pair).wait_send()

        return 0

    lax.fori_loop(0, RB, row_sent, 0)


def exchange_call(child, maptile, front, pattern):
    dma = pltpu.SemaphoreType.DMA
    shape = jax.ShapeDtypeStruct
    return pl.pallas_call(
        exchange,
        out_shape=(
            shape((NL, B, B), F32), shape((8, B), jnp.int32),
            shape((RB, B, W), F32), shape((NR, B, W), F32),
        ),
        in_specs=[HBM, HBM, HBM, SMEM],
        out_specs=(HBM,) * 4,
        scratch_shapes=[
            pltpu.VMEM((NL, B, B), F32), pltpu.VMEM((RB * B, W), F32),
            pltpu.VMEM((RB, B, W), F32), pltpu.VMEM((NL, 8, B), jnp.int32),
            pltpu.VMEM((8, B), jnp.int32), pltpu.SMEM((8, B), jnp.int32),
            dma((NL,)), dma((NL,)), dma((NL,)), dma((NL,)), dma((RB, 2)), dma((RB,)),
            dma((NR, NY)), dma((NR, 2)), dma((NR, NY)), dma((NR, NY)), dma((16 + NR,)),
        ],
        compiler_params=pltpu.CompilerParams(
            collective_id=0, has_side_effects=True, vmem_limit_bytes=32 << 20
        ),
    )(child, maptile, front, pattern)


def factor_block(s):
    sub = lax.broadcasted_iota(jnp.int32, (8, B), 0)
    lane = lax.broadcasted_iota(jnp.int32, (8, B), 1)
    groups = B // 8

    def down(value, i):
        return jnp.broadcast_to(value[i : i + 1, :], (8, B))

    left = [s[8 * g : 8 * g + 8, :] for g in range(groups)]
    right = [(lane == sub + 8 * g).astype(F32) for g in range(groups)]
    upper, inverse = [], []
    for p in range(groups):
        cols = [
            [jnp.broadcast_to(left[g][:, 8 * p + i : 8 * p + i + 1], (8, B)) for g in range(p, groups)]
            for i in range(8)
        ]
        done_l = jnp.zeros((8, B), F32)
        done_r = jnp.zeros((8, B), F32)
        for i in range(8):
            scale = lax.rsqrt(down(cols[i][0], i))
            col = [value * scale for value in cols[i]]
            row_l = down(left[p], i) * scale
            row_r = down(right[p], i) * scale
            done_l = jnp.where(sub == i, row_l, done_l)
            done_r = jnp.where(sub == i, row_r, done_r)
            for k in range(i + 1, 8):
                at = down(col[0], k)
                cols[k] = [v - w * at for v, w in zip(cols[k], col)]
            for g in range(p, groups):
                left[g] = left[g] - col[g - p] * row_l
                right[g] = right[g] - col[g - p] * row_r
        upper.append(jnp.where(lane >= sub + 8 * p, done_l, 0.0))
        inverse.append(done_r)
    return jnp.concatenate(upper, 0), jnp.concatenate(inverse, 0)


def dot_exact(a, b, contract):
    return lax.dot_general(
        a, b, (contract, ((), ())), precision=lax.Precision.HIGHEST, preferred_element_type=F32
    )


NT = ((1,), (1,))
NN = ((1,), (0,))


def factor_lead(work, pivots, inv):
    r = lax.broadcasted_iota(jnp.int32, (B, B), 0)
    c = lax.broadcasted_iota(jnp.int32, (B, B), 1)
    inv[...] = jnp.zeros_like(inv)
    for k in range(PANELS):
        at = slice(B * k, B * k + B)
        pivot = work[at, at]
        upper, inverse = factor_block(jnp.where(r >= c, pivot, pivot.T))
        pivots[k] = upper.T
        inv[at, at] = inverse
        if k < PANELS - 1:
            below = slice(B * k + B, W)
            lower = dot_exact(work[below, at], inverse, NT)
            work[below, at] = lower
            work[below, below] = work[below, below] - dot_exact(lower, lower, NT)
    for k in range(1, PANELS):
        at, before = slice(B * k, B * k + B), slice(0, B * k)
        inv[at, before] = -dot_exact(inv[at, at], dot_exact(work[at, before], inv[before, before], NN), NN)


def halves(a):
    high = a.astype(BF16)
    return high, (a - high.astype(F32)).astype(BF16)


def dot_split(a, b):
    (ah, al), (bh, bl) = a, b
    dot = functools.partial(
        lax.dot_general, dimension_numbers=(NT, ((), ())), preferred_element_type=F32
    )
    return dot(ah, bh) + (dot(al, bh) + dot(ah, bl))


STEP = 2


def finish_kernel(
    code, pattern, front, rows, match, arrived, out,
    work, pivots, inv, inv_h, inv_l, across_h, across_l,
):
    n = pl.program_id(0)
    d = lax.axis_index("leaf")
    f = lax.axis_index("front")

    @pl.when(n == 0)
    def _():
        for k in range(PANELS):
            work[B * k : B * k + B, :] = match[CB + k]
        factor_lead(work, pivots, inv)
        inv_h[...], inv_l[...] = halves(inv[...])
        for i in range(0, CB, STEP):
            part = match[i : i + STEP].reshape(STEP * B, W)
            lower = dot_split(halves(part), (inv_h[...], inv_l[...]))
            at = slice(i * B, (i + STEP) * B)
            across_h[at, :], across_l[at, :] = halves(lower)

    lower = dot_split(halves(rows[...].reshape(STEP * B, W)), (inv_h[...], inv_l[...]))
    product = dot_split(halves(lower), (across_h[...], across_l[...]))
    for rr in range(STEP):
        r = n * STEP + rr
        r_glob = d * RB + r
        rs = slice(rr * B, rr * B + B)
        for c in range(CB):
            c_glob = f * CB + c
            cs = slice(c * B, c * B + B)
            t = code[0, r * CB + c]
            keep = ((pattern[r, c] == 1) | (r_glob == c_glob)) & (r_glob >= c_glob)
            active = (r_glob >= c_glob) & (c_glob >= PANELS)
            block = arrived[jnp.maximum(t - 1, 0)]
            value = (front[rs, cs] + block * (t > 0).astype(F32)) * keep.astype(F32)
            out[rs, cs] = value - product[rs, cs] * active.astype(F32)

        @pl.when(f == 0)
        def _():
            for c in range(PANELS):
                cs = slice(c * B, c * B + B)
                solved = lower[rs, cs] * (r_glob > c).astype(F32)
                out[rs, cs] = solved + pivots[c] * (r_glob == c).astype(F32)


def finish_call(code, pattern, front, rows, match, arrived):
    whole = lambda *shape: pl.BlockSpec(shape, lambda n, *_: (0,) * len(shape))
    return pl.pallas_call(
        finish_kernel,
        out_shape=jax.ShapeDtypeStruct(front.shape, F32),
        grid_spec=pltpu.PrefetchScalarGridSpec(
            num_scalar_prefetch=2,
            grid=(RB // STEP,),
            in_specs=[
                pl.BlockSpec((STEP * B, CB * B), lambda n, *_: (n, 0)),
                pl.BlockSpec((STEP, B, W), lambda n, *_: (n, 0, 0)),
                whole(NR, B, W),
                whole(NL, B, B),
            ],
            out_specs=pl.BlockSpec((STEP * B, CB * B), lambda n, *_: (n, 0)),
            scratch_shapes=[
                pltpu.VMEM((W, W), F32), pltpu.VMEM((PANELS, B, B), F32), pltpu.VMEM((W, W), F32),
                pltpu.VMEM((W, W), BF16), pltpu.VMEM((W, W), BF16),
                pltpu.VMEM((CB * B, W), BF16), pltpu.VMEM((CB * B, W), BF16),
            ],
        ),
        compiler_params=pltpu.CompilerParams(vmem_limit_bytes=56 << 20),
    )(code, pattern, front, rows, match, arrived)


def body(front, child_blocks, child_map, pattern):
    child = child_blocks.reshape(NL, B, B)
    maptile = jnp.broadcast_to(child_map.reshape(NL, 1, 1), (NL, 8, B))
    arrived, code, rows, match = exchange_call(child, maptile, front, pattern)
    return finish_call(code, pattern, front, rows, match, arrived)


def solution(mesh):
    placed = (
        P("leaf", "front"),
        P("leaf", None, None, "front"),
        P("leaf", None, "front"),
        P("leaf", "front"),
    )
    return jax.shard_map(
        body, mesh=mesh, in_specs=placed, out_specs=P("leaf", "front"), check_vma=False
    )
```

time: 1690 us -> 273 us (0.16)
  the two profiles are of different devices: /device:TPU:167 before, /device:TPU:146 now
where the time goes in v1:
time: 273 us
  Pallas kernels  262 us (96%)
  local copies, waits for them, and re-layouts  10.7 us (4%)
    pallas_call x1, Pallas kernels, exchange_call(): pl.pallas_call(exchange, out_shape=(shape((NL, B, B), F32), shape((8, B),...  228 us
    pallas_call x1, Pallas kernels, finish_call(): pl.pallas_call(finish_kernel, out_shape=jax.ShapeDtypeStruct(front.shape,...  34.2 us
    unnamed x15, local copies, waits for them, and re-layouts  9.92 us

profile of v1, /device:TPU:146, one launch (start us, length us, event | category | flops | bytes accessed | tf_op | source)
XLA Modules:
  0.0 272.6 jit_solution(4369748421725911947)
XLA Ops:
  0.0 0.8 copy.5.pattern
  0.8 0.0 copy-start.5
  0.8 0.7 broadcast_in_dim.8.maptile
  1.5 0.0 copy-start
  1.5 2.5 copy-done
  4.0 0.0 copy-start.3
  4.0 1.6 copy-done.3
  5.6 227.6 %shard_map.46 = (f32[32,128,128]{2,1,0:T(8,128)S(1)}, s32[8,128]{1,0:T(8,128)S(1)}, f32[10,128,512]{2,1,0:T(8,128)S(1)}, f32[12,128,512]{2,1,0:T(8,128)S(1)}) custom-call(f32[32,128,128]{2,1,0:T(8,128)S(1)} %bitcast.2, s32[32,8,128]{2,1,0:T(8,128)S(1)} %broadcast_in_dim.8.maptile, f32[1280,1024]{1,0:T(8,128)S(1)} %copy-done, s32[10,8]{1,0:T(8,128)S(1)} %copy.5.pattern), custom_call_target="tpu_custom_call" | custom-call | tf_op jit(solution)/shard_map/pallas_call | solution.py:327
  233.3 0.0 copy-done.5
  233.3 0.0 copy-start.1
  233.3 1.6 copy-done.1
  234.9 0.0 copy-start.2
  234.9 1.5 copy-done.2
  236.5 0.0 copy-start.4
  236.5 1.3 copy-done.4
  237.8 0.0 copy-start.6
  237.8 0.6 copy-done.6
  238.4 34.2 %shard_map.47 = f32[1280,1024]{1,0:T(8,128)} custom-call(s32[8,128]{1,0:T(8,128)} %copy-done.6, s32[10,8]{1,0:T(8,128)} %copy-done.5, f32[1280,1024]{1,0:T(8,128)} %front.3, f32[10,128,512]{2,1,0:T(8,128)} %copy-done.2, f32[12,128,512]{2,1,0:T(8,128)} %copy-done.1, f32[32,128,128]{2,1,0:T(8,128)} %copy-done.4), custom_call_target="tpu_custom_call" | custom-call | tf_op jit(solution)/shard_map/pallas_call | solution.py:476
Async XLA Ops:
  0.8 232.5 %copy-start.5 = (s32[10,8]{1,0:T(8,128)}, s32[10,8]{1,0:T(8,128)S(1)}, u32[]{:S(2)}) copy-start(s32[10,8]{1,0:T(8,128)S(1)} %copy.5.pattern) | copy-start | bytes 964
  1.5 2.5 copy-start
  4.0 1.6 copy-start.3
  233.3 1.6 copy-start.1
  234.9 1.5 copy-start.2
  236.5 1.3 copy-start.4
  237.8 0.6 copy-start.6

commit v2 on v1

v2 whole, which is shorter than its diff:
```python
import functools

import jax
import jax.numpy as jnp
from jax import lax
from jax.experimental import pallas as pl
from jax.experimental.pallas import tpu as pltpu
from jax.sharding import PartitionSpec as P

B = 128
RB = 10
CB = 8
PANELS = 4
W = PANELS * B
NL = 32
NF = 8
NY = 4
NZ = 8
PIECE = B // NY
LR = 3
NR = CB + LR
CHUNK = B // 2
NC = RB * B // CHUNK
F32 = jnp.float32
BF16 = jnp.bfloat16
MESH = pl.DeviceIdType.MESH
HBM = pl.BlockSpec(memory_space=pl.ANY)
SMEM = pl.BlockSpec(memory_space=pltpu.SMEM)
VMEM = pl.BlockSpec(memory_space=pltpu.VMEM)


def exchange(
    child, maptile, front, pattern,
    arrived_out, code, rows_out, match_out, pivots_out,
    child_v, arrived, front_v, rows, match, work, inv, pivots, map_v, code_v, code_s,
    a_send, a_recv, m_send, m_recv, x_send, x_recv, l_send, l_recv, t_send, t_recv,
    q_recv, qz_send, qy_send, qa_send, local,
):
    d = lax.axis_index("leaf")
    f = lax.axis_index("front")
    z, y = d // NY, d % NY
    x, core = f // 2, f % 2

    child_in = pltpu.make_async_copy(child, child_v, local.at[4])
    child_in.start()
    front_in = pltpu.make_async_copy(front.at[:, pl.ds(0, W)], front_v, local.at[3])

    @pl.when(f == 0)
    def _():
        front_in.start()

    barrier = pltpu.get_barrier_semaphore()

    def greet_leaf(k, _):
        pl.semaphore_signal(
            barrier, inc=1, device_id=(lax.rem(d + k, NL), f), device_id_type=MESH
        )
        return 0

    def greet_front(k, _):
        pl.semaphore_signal(
            barrier, inc=1, device_id=(d, lax.rem(f + k, NF)), device_id_type=MESH
        )
        return 0

    lax.fori_loop(1, NL, greet_leaf, 0)
    lax.fori_loop(1, NF, greet_front, 0)
    pl.semaphore_wait(barrier, NL - 1 + NF - 1)

    child_in.wait()

    def block_copy(k):
        to = lax.rem(d + k, NL)
        return pltpu.make_async_remote_copy(
            src_ref=child_v.at[to], dst_ref=arrived.at[d], send_sem=a_send.at[k],
            recv_sem=a_recv.at[k], device_id=(to, f), device_id_type=MESH,
        )

    def map_copy(k):
        to = lax.rem(d + k, NL)
        return pltpu.make_async_remote_copy(
            src_ref=maptile.at[to], dst_ref=map_v.at[d], send_sem=m_send.at[k],
            recv_sem=m_recv.at[k], device_id=(to, f), device_id_type=MESH,
        )

    def block_in(k):
        frm = lax.rem(d - k + NL, NL)
        return pltpu.make_async_remote_copy(
            src_ref=child_v.at[frm], dst_ref=arrived.at[frm], send_sem=a_send.at[k],
            recv_sem=a_recv.at[k], device_id=(frm, f), device_id_type=MESH,
        )

    def map_in(k):
        frm = lax.rem(d - k + NL, NL)
        return pltpu.make_async_remote_copy(
            src_ref=maptile.at[frm], dst_ref=map_v.at[frm], send_sem=m_send.at[k],
            recv_sem=m_recv.at[k], device_id=(frm, f), device_id_type=MESH,
        )

    own_block = pltpu.make_async_copy(child_v.at[d], arrived.at[d], local.at[0])
    own_map = pltpu.make_async_copy(maptile.at[d], map_v.at[d], local.at[1])

    def send_blocks():
        def step(k, _):
            map_copy(k).start()
            block_copy(k).start()
            return 0

        lax.fori_loop(1, NL, step, 0)

    def receive_blocks():
        def step(k, _):
            map_in(k).wait_recv()
            block_in(k).wait_recv()
            return 0

        lax.fori_loop(1, NL, step, 0)
        own_block.wait()
        own_map.wait()
        lane = lax.broadcasted_iota(jnp.int32, (8, B), 1)

        def latest(s, total):
            return jnp.maximum(total, jnp.where(map_v[s] == lane, s + 1, 0))

        code_v[...] = lax.fori_loop(0, NL, latest, jnp.zeros((8, B), jnp.int32))
        pltpu.make_async_copy(code_v, code, local.at[2]).start()
        pltpu.make_async_copy(arrived, arrived_out, local.at[0]).start()

    own_block.start()
    own_map.start()

    @pl.when(f != 1)
    def _():
        send_blocks()

    def chunk_of(j):
        return rows.at[pl.ds(pl.multiple_of(j * CHUNK, CHUNK), CHUNK)]

    def chunk_copy(j, to, way):
        return pltpu.make_async_remote_copy(
            src_ref=chunk_of(j), dst_ref=chunk_of(j), send_sem=x_send.at[j, way],
            recv_sem=x_recv.at[j], device_id=(d, to), device_id_type=MESH,
        )

    def root_next(j):
        return jnp.where(j % 2 == 0, 2, NF - 1)

    @pl.when(f == 0)
    def _():
        receive_blocks()
        to_smem = pltpu.make_async_copy(code_v, code_s, local.at[3])
        front_in.wait()
        to_smem.start()
        to_smem.wait()

        def form(r, _):
            r_glob = d * RB + r
            at = pl.ds(pl.multiple_of(r * B, B), B)
            for c in range(PANELS):
                t = code_s[0, r * CB + c]
                block = arrived[jnp.maximum(t - 1, 0)]
                has = (t > 0).astype(F32)
                keep = ((pattern[r, c] == 1) | (r_glob == c)) & (r_glob >= c)
                raw = front_v[at, c * B : (c + 1) * B]
                rows[at, c * B : (c + 1) * B] = (raw + block * has) * keep.astype(F32)
            for h in range(2):
                j = 2 * r + h
                chunk_copy(j, root_next(j), 0).start()
                chunk_copy(j, 1, 1).start()
            return 0

        lax.fori_loop(0, RB, form, 0)

    pair = f + 1 - 2 * core
    onward = f + 2 - 4 * core
    has_onward = ((core == 0) & (x < 3)) | ((core == 1) & (x > 1))

    @pl.when(f != 0)
    def _():
        def passing(n, _):
            j = 2 * n + core
            chunk_copy(j, 0, 0).wait_recv()

            @pl.when(f >= 2)
            def _():
                @pl.when(has_onward)
                def _():
                    chunk_copy(j, onward, 0).start()

                chunk_copy(j, pair, 1).start()

            return 0

        def ending(n, _):
            chunk_copy(2 * n + 1 - core, 0, 0).wait_recv()
            return 0

        lax.fori_loop(0, NC // 2, passing, 0)
        lax.fori_loop(0, NC // 2, ending, 0)

    @pl.when(f == 1)
    def _():
        send_blocks()

    def where_from(i, lead):
        r = 0 if lead else f * CB + i
        source = r // RB
        zs, ys = source // NY, source % NY
        return r % RB, ys, lax.rem(z - zs + NZ, NZ)

    def row_of(ref, i):
        return ref.at[pl.ds(pl.multiple_of(i * B, B), B)]

    def piece_of(ref, i, q):
        return ref.at[pl.ds(pl.multiple_of(i * B + q * PIECE, PIECE), PIECE)]

    def piece_copy(src, i, q, to_z, to_y, sem):
        return pltpu.make_async_remote_copy(
            src_ref=src, dst_ref=piece_of(match, i, q), send_sem=sem,
            recv_sem=q_recv.at[i, q], device_id=(to_z * NY + to_y, f), device_id_type=MESH,
        )

    def z_copy(src, i, up):
        to = lax.rem(z + (1 if up else NZ - 1), NZ)
        return piece_copy(src, i, y, to, y, qz_send.at[i, 0 if up else 1])

    def match_row(i, act, lead):
        r_loc, ys, zr = where_from(i, lead)
        held, r_at = (match, i) if lead else (rows, r_loc)
        at_source = (zr == 0) & (y == ys)

        @pl.when(at_source)
        def _():
            mine = piece_of(held, r_at, y)
            act(z_copy(mine, i, True))
            act(z_copy(mine, i, False))
            for k in range(1, NY):
                q = lax.rem(y + k, NY)
                act(piece_copy(piece_of(held, r_at, q), i, q, z, q, qa_send.at[i, k]))
            for k in range(1, NY):
                q = lax.rem(y + k, NY)
                act(piece_copy(mine, i, y, z, q, qy_send.at[i, k]))
            if not lead:
                act(
                    pltpu.make_async_copy(row_of(rows, r_loc), row_of(match, i), local.at[16 + i]),
                    here=True,
                )

        @pl.when(jnp.logical_not(at_source))
        def _():
            mine = piece_of(match, i, y)
            act(None, i, y)

            @pl.when(zr < NZ // 2)
            def _():
                act(z_copy(mine, i, True))

            @pl.when((zr == 0) | (zr > NZ // 2 + 1))
            def _():
                act(z_copy(mine, i, False))

            for k in range(1, NY):
                q = lax.rem(y + k, NY)

                @pl.when((zr != 0) | (q != ys))
                def _():
                    act(piece_copy(mine, i, y, z, q, qy_send.at[i, k]))

                act(None, i, q, late=True)

    def piece_in(i, q):
        piece_copy(piece_of(match, i, q), i, q, z, lax.rem(y + 1, NY), qy_send.at[i, 1]).wait_recv()

    def begin(copy, i=None, q=None, late=False, here=False):
        if copy is not None:
            copy.start()
        elif not late:
            piece_in(i, q)

    def finish(copy, i=None, q=None, late=False, here=False):
        if copy is None:
            if late:
                piece_in(i, q)
        elif here:
            copy.wait()
        else:
            copy.wait_send()

    def run(act, first, last, lead):
        def step(i, _):
            match_row(i, act, lead)
            return 0

        lax.fori_loop(first, last, step, 0)

    def lead_copy(i, to, way):
        return pltpu.make_async_remote_copy(
            src_ref=row_of(match, i), dst_ref=row_of(match, i), send_sem=l_send.at[i - CB, way],
            recv_sem=l_recv.at[i - CB], device_id=(d, to), device_id_type=MESH,
        )

    def twin_copy(i, to):
        return pltpu.make_async_remote_copy(
            src_ref=row_of(match, i), dst_ref=row_of(match, i), send_sem=t_send.at[i - CB],
            recv_sem=t_recv.at[i - CB], device_id=(d, to), device_id_type=MESH,
        )

    keep_rows = pltpu.make_async_copy(rows, rows_out, local.at[7])
    keep_rows.start()
    run(begin, 0, CB, False)
    is_root = (d == 0) & (f == 0)
    keep_pivots = pltpu.make_async_copy(pivots, pivots_out, local.at[6])

    @pl.when(is_root)
    def _():
        work[...] = rows[0:W, :]
        factor_lead(work, pivots, inv)
        keep_pivots.start()
        match[CB * B :, :] = jnp.zeros((LR * B, W), F32)
        for i in range(PANELS):
            for j in range(i + 1):
                n = i * (i + 1) // 2 + j
                at = (CB + n // PANELS) * B
                to = n % PANELS * B
                match[at : at + B, to : to + B] = inv[i * B : i * B + B, j * B : j * B + B]
        for i in range(CB, NR):
            lead_copy(i, 2, 0).start()
            lead_copy(i, NF - 2, 1).start()

    @pl.when((d == 0) & (core == 0) & (f != 0))
    def _():
        for i in range(CB, NR):
            lead_copy(i, 0, 0).wait_recv()

            @pl.when(f == 2)
            def _():
                lead_copy(i, 4, 0).start()

    @pl.when(core == 0)
    def _():
        run(begin, CB, NR, True)

    @pl.when(f != 0)
    def _():
        receive_blocks()

    run(finish, 0, CB, False)

    @pl.when(core == 0)
    def _():
        run(finish, CB, NR, True)
        for i in range(CB, NR):
            twin_copy(i, f + 1).start()
        for i in range(CB, NR):
            twin_copy(i, f + 1).wait_send()

    @pl.when(core == 1)
    def _():
        for i in range(CB, NR):
            twin_copy(i, f - 1).wait_recv()

    keep_match = pltpu.make_async_copy(match, match_out, local.at[5])
    keep_match.start()

    @pl.when(is_root)
    def _():
        for i in range(CB, NR):
            lead_copy(i, 2, 0).wait_send()
            lead_copy(i, NF - 2, 1).wait_send()
        keep_pivots.wait()

    @pl.when((d == 0) & (f == 2))
    def _():
        for i in range(CB, NR):
            lead_copy(i, 4, 0).wait_send()

    def sent(k, _):
        map_copy(k).wait_send()
        block_copy(k).wait_send()
        return 0

    lax.fori_loop(1, NL, sent, 0)

    @pl.when(f == 0)
    def _():
        def chunk_sent(j, _):
            chunk_copy(j, root_next(j), 0).wait_send()
            chunk_copy(j, 1, 1).wait_send()
            return 0

        lax.fori_loop(0, NC, chunk_sent, 0)

    @pl.when(f >= 2)
    def _():
        def chunk_sent(n, _):
            j = 2 * n + core

            @pl.when(has_onward)
            def _():
                chunk_copy(j, onward, 0).wait_send()

            chunk_copy(j, pair, 1).wait_send()
            return 0

        lax.fori_loop(0, NC // 2, chunk_sent, 0)

    keep_rows.wait()
    keep_match.wait()
    pltpu.make_async_copy(code_v, code, local.at[2]).wait()
    pltpu.make_async_copy(arrived, arrived_out, local.at[0]).wait()


def exchange_call(child, maptile, front, pattern):
    dma = pltpu.SemaphoreType.DMA
    shape = jax.ShapeDtypeStruct
    return pl.pallas_call(
        exchange,
        out_shape=(
            shape((NL, B, B), F32), shape((8, B), jnp.int32),
            shape((RB * B, W), F32), shape((NR * B, W), F32), shape((PANELS, B, B), F32),
        ),
        in_specs=[HBM, HBM, HBM, SMEM],
        out_specs=(HBM,) * 5,
        scratch_shapes=[
            pltpu.VMEM((NL, B, B), F32), pltpu.VMEM((NL, B, B), F32),
            pltpu.VMEM((RB * B, W), F32), pltpu.VMEM((RB * B, W), F32),
            pltpu.VMEM((NR * B, W), F32), pltpu.VMEM((W, W), F32), pltpu.VMEM((W, W), F32),
            pltpu.VMEM((PANELS, B, B), F32), pltpu.VMEM((NL, 8, B), jnp.int32),
            pltpu.VMEM((8, B), jnp.int32), pltpu.SMEM((8, B), jnp.int32),
            dma((NL,)), dma((NL,)), dma((NL,)), dma((NL,)), dma((NC, 2)), dma((NC,)),
            dma((LR, 2)), dma((LR,)), dma((LR,)), dma((LR,)),
            dma((NR, NY)), dma((NR, 2)), dma((NR, NY)), dma((NR, NY)), dma((16 + NR,)),
        ],
        compiler_params=pltpu.CompilerParams(
            collective_id=0, has_side_effects=True, vmem_limit_bytes=56 << 20
        ),
    )(child, maptile, front, pattern)


def factor_block(s):
    sub = lax.broadcasted_iota(jnp.int32, (8, B), 0)
    lane = lax.broadcasted_iota(jnp.int32, (8, B), 1)
    groups = B // 8

    def down(value, i):
        return jnp.broadcast_to(value[i : i + 1, :], (8, B))

    left = [s[8 * g : 8 * g + 8, :] for g in range(groups)]
    right = [(lane == sub + 8 * g).astype(F32) for g in range(groups)]
    upper, inverse = [], []
    for p in range(groups):
        cols = [
            [jnp.broadcast_to(left[g][:, 8 * p + i : 8 * p + i + 1], (8, B)) for g in range(p, groups)]
            for i in range(8)
        ]
        done_l = jnp.zeros((8, B), F32)
        done_r = jnp.zeros((8, B), F32)
        for i in range(8):
            scale = lax.rsqrt(down(cols[i][0], i))
            col = [value * scale for value in cols[i]]
            row_l = down(left[p], i) * scale
            row_r = down(right[p], i) * scale
            done_l = jnp.where(sub == i, row_l, done_l)
            done_r = jnp.where(sub == i, row_r, done_r)
            for k in range(i + 1, 8):
                at = down(col[0], k)
                cols[k] = [v - w * at for v, w in zip(cols[k], col)]
            for g in range(p, groups):
                left[g] = left[g] - col[g - p] * row_l
                right[g] = right[g] - col[g - p] * row_r
        upper.append(jnp.where(lane >= sub + 8 * p, done_l, 0.0))
        inverse.append(done_r)
    return jnp.concatenate(upper, 0), jnp.concatenate(inverse, 0)


def dot_exact(a, b, contract):
    return lax.dot_general(
        a, b, (contract, ((), ())), precision=lax.Precision.HIGHEST, preferred_element_type=F32
    )


NT = ((1,), (1,))
NN = ((1,), (0,))


def factor_lead(work, pivots, inv):
    r = lax.broadcasted_iota(jnp.int32, (B, B), 0)
    c = lax.broadcasted_iota(jnp.int32, (B, B), 1)
    row_block = lax.broadcasted_iota(jnp.int32, (W, B), 0) // B
    col_block = lax.broadcasted_iota(jnp.int32, (B, W), 1) // B
    inv[...] = jnp.zeros_like(inv)

    def panel(k, _):
        at = pl.ds(pl.multiple_of(k * B, B), B)
        pivot = work[at, at]
        upper, inverse = factor_block(jnp.where(r >= c, pivot, pivot.T))
        pivots[k] = upper.T
        lower = jnp.where(row_block > k, dot_exact(work[:, at], inverse, NT), 0.0)
        before = jnp.where(col_block < k, work[at, :], 0.0)
        inv[at, :] = -dot_exact(inverse, dot_exact(before, inv[...], NN), NN)
        inv[at, at] = inverse
        work[...] = work[...] - dot_exact(lower, lower, NT)
        work[:, at] = lower
        return 0

    lax.fori_loop(0, PANELS, panel, 0)


def halves(a):
    high = a.astype(BF16)
    return high, (a - high.astype(F32)).astype(BF16)


def dot_split(a, b):
    (ah, al), (bh, bl) = a, b
    dot = functools.partial(
        lax.dot_general, dimension_numbers=(NT, ((), ())), preferred_element_type=F32
    )
    return dot(ah, bh) + (dot(al, bh) + dot(ah, bl))


STEP = 2


def finish_kernel(
    code, pattern, front, rows, match, pivots, arrived, out,
    inv_h, inv_l, across_h, across_l,
):
    n = pl.program_id(0)
    d = lax.axis_index("leaf")
    f = lax.axis_index("front")

    @pl.when(n == 0)
    def _():
        inv_h[...] = jnp.zeros_like(inv_h)
        inv_l[...] = jnp.zeros_like(inv_l)
        for i in range(PANELS):
            for j in range(i + 1):
                k = i * (i + 1) // 2 + j
                ks, ls = (CB + k // PANELS) * B, k % PANELS * B
                at, to = slice(i * B, i * B + B), slice(j * B, j * B + B)
                inv_h[at, to], inv_l[at, to] = halves(match[ks : ks + B, ls : ls + B])
        for i in range(0, CB, STEP):
            at = slice(i * B, (i + STEP) * B)
            lower = dot_split(halves(match[at, :]), (inv_h[...], inv_l[...]))
            across_h[at, :], across_l[at, :] = halves(lower)

    lower = dot_split(halves(rows[...]), (inv_h[...], inv_l[...]))
    product = dot_split(halves(lower), (across_h[...], across_l[...]))
    for rr in range(STEP):
        r = n * STEP + rr
        r_glob = d * RB + r
        rs = slice(rr * B, rr * B + B)
        for c in range(CB):
            c_glob = f * CB + c
            cs = slice(c * B, c * B + B)
            t = code[0, r * CB + c]
            keep = ((pattern[r, c] == 1) | (r_glob == c_glob)) & (r_glob >= c_glob)
            active = (r_glob >= c_glob) & (c_glob >= PANELS)
            block = arrived[jnp.maximum(t - 1, 0)]
            value = (front[rs, cs] + block * (t > 0).astype(F32)) * keep.astype(F32)
            out[rs, cs] = value - product[rs, cs] * active.astype(F32)

        @pl.when(f == 0)
        def _():
            for c in range(PANELS):
                cs = slice(c * B, c * B + B)
                out[rs, cs] = lower[rs, cs] * (r_glob > c).astype(F32)

                @pl.when(r_glob == c)
                def _():
                    out[rs, cs] = pivots[c]


def finish_call(code, pattern, front, rows, match, pivots, arrived):
    whole = lambda *shape: pl.BlockSpec(shape, lambda n, *_: (0,) * len(shape))
    return pl.pallas_call(
        finish_kernel,
        out_shape=jax.ShapeDtypeStruct(front.shape, F32),
        grid_spec=pltpu.PrefetchScalarGridSpec(
            num_scalar_prefetch=2,
            grid=(RB // STEP,),
            in_specs=[
                pl.BlockSpec((STEP * B, CB * B), lambda n, *_: (n, 0)),
                pl.BlockSpec((STEP * B, W), lambda n, *_: (n, 0)),
                whole(NR * B, W),
                whole(PANELS, B, B),
                whole(NL, B, B),
            ],
            out_specs=pl.BlockSpec((STEP * B, CB * B), lambda n, *_: (n, 0)),
            scratch_shapes=[
                pltpu.VMEM((W, W), BF16), pltpu.VMEM((W, W), BF16),
                pltpu.VMEM((CB * B, W), BF16), pltpu.VMEM((CB * B, W), BF16),
            ],
        ),
        compiler_params=pltpu.CompilerParams(vmem_limit_bytes=56 << 20),
    )(code, pattern, front, rows, match, pivots, arrived)


def body(front, child_blocks, child_map, pattern):
    child = child_blocks.reshape(NL, B, B)
    maptile = jnp.broadcast_to(child_map.reshape(NL, 1, 1), (NL, 8, B))
    arrived, code, rows, match, pivots = exchange_call(child, maptile, front, pattern)
    return finish_call(code, pattern, front, rows, match, pivots, arrived)


def solution(mesh):
    placed = (
        P("leaf", "front"),
        P("leaf", None, None, "front"),
        P("leaf", None, "front"),
        P("leaf", "front"),
    )
    return jax.shard_map(
        body, mesh=mesh, in_specs=placed, out_specs=P("leaf", "front"), check_vma=False
    )
```

time: 273 us -> 159 us (0.58)
  the two profiles are of different devices: /device:TPU:146 before, /device:TPU:133 now
where the time goes in v2:
time: 159 us; the launch traced here: 158 us
  Pallas kernels  156 us (98%)
  local copies, waits for them, and re-layouts  2.76 us (2%)
    pallas_call x1, Pallas kernels, exchange_call(): pl.pallas_call(exchange, out_shape=(shape((NL, B, B), F32), shape((8, B),...  140 us
    pallas_call x1, Pallas kernels, finish_call(): pl.pallas_call(finish_kernel, out_shape=jax.ShapeDtypeStruct(front.shape,...  15.2 us

profile of v2, /device:TPU:133, one launch (start us, length us, event | category | flops | bytes accessed | tf_op | source)
XLA Modules:
  0.0 158.4 jit_solution(12887584463327039284)
XLA Ops:
  0.0 1.4 copy.5.pattern
  1.4 1.4 broadcast_in_dim.8.maptile
  2.8 140.5 %shard_map.46 = (f32[32,128,128]{2,1,0:T(8,128)}, s32[8,128]{1,0:T(8,128)}, f32[1280,512]{1,0:T(8,128)}, f32[1408,512]{1,0:T(8,128)}, f32[4,128,128]{2,1,0:T(8,128)}) custom-call(f32[32,128,128]{2,1,0:T(8,128)} %bitcast.2, s32[32,8,128]{2,1,0:T(8,128)} %broadcast_in_dim.8.maptile, f32[1280,1024]{1,0:T(8,128)} %front.3, s32[10,8]{1,0:T(8,128)} %copy.5.pattern), custom_call_target="tpu_custom_call" | custom-call | tf_op jit(solution)/shard_map/pallas_call | solution.py:416
  143.3 15.2 %shard_map.47 = f32[1280,1024]{1,0:T(8,128)} custom-call(s32[8,128]{1,0:T(8,128)} %get-tuple-element.10.code, s32[10,8]{1,0:T(8,128)} %copy.5.pattern, f32[1280,1024]{1,0:T(8,128)} %front.3, f32[1280,512]{1,0:T(8,128)} %get-tuple-element.11.rows, f32[1408,512]{1,0:T(8,128)} %get-tuple-element.12.match, f32[4,128,128]{2,1,0:T(8,128)} %get-tuple-element.13.pivots, ...), custom_call_target="tpu_custom_call" | custom-call | tf_op jit(solution)/shard_map/pallas_call | solution.py:577

commit v3 on v2

--- a/solution.py
+++ b/solution.py
@@ -17,8 +17,12 @@
 NY = 4
 NZ = 8
 PIECE = B // NY
-LR = 3
+LR = PANELS
 NR = CB + LR
+NS = -(-NF * CB // RB)
+LAG = 2
+RELAY_LAG = 1
+LEAD_TURN = CB
 CHUNK = B // 2
 NC = RB * B // CHUNK
 F32 = jnp.float32
@@ -69,32 +73,28 @@
 
     child_in.wait()
 
-    def block_copy(k):
-        to = lax.rem(d + k, NL)
-        return pltpu.make_async_remote_copy(
-            src_ref=child_v.at[to], dst_ref=arrived.at[d], send_sem=a_send.at[k],
-            recv_sem=a_recv.at[k], device_id=(to, f), device_id_type=MESH,
-        )
-
-    def map_copy(k):
-        to = lax.rem(d + k, NL)
-        return pltpu.make_async_remote_copy(
-            src_ref=maptile.at[to], dst_ref=map_v.at[d], send_sem=m_send.at[k],
-            recv_sem=m_recv.at[k], device_id=(to, f), device_id_type=MESH,
-        )
-
-    def block_in(k):
-        frm = lax.rem(d - k + NL, NL)
-        return pltpu.make_async_remote_copy(
-            src_ref=child_v.at[frm], dst_ref=arrived.at[frm], send_sem=a_send.at[k],
-            recv_sem=a_recv.at[k], device_id=(frm, f), device_id_type=MESH,
-        )
-
-    def map_in(k):
-        frm = lax.rem(d - k + NL, NL)
-        return pltpu.make_async_remote_copy(
-            src_ref=maptile.at[frm], dst_ref=map_v.at[frm], send_sem=m_send.at[k],
-            recv_sem=m_recv.at[k], device_id=(frm, f), device_id_type=MESH,
+    def block_copy(to):
+        return pltpu.make_async_remote_copy(
+            src_ref=child_v.at[to], dst_ref=arrived.at[d], send_sem=a_send.at[to],
+            recv_sem=a_recv.at[d], device_id=(to, f), device_id_type=MESH,
+        )
+
+    def map_copy(to):
+        return pltpu.make_async_remote_copy(
+            src_ref=maptile.at[to], dst_ref=map_v.at[d], send_sem=m_send.at[to],
+            recv_sem=m_recv.at[d], device_id=(to, f), device_id_type=MESH,
+        )
+
+    def block_in(frm):
+        return pltpu.make_async_remote_copy(
+            src_ref=child_v.at[frm], dst_ref=arrived.at[frm], send_sem=a_send.at[frm],
+            recv_sem=a_recv.at[frm], device_id=(frm, f), device_id_type=MESH,
+        )
+
+    def map_in(frm):
+        return pltpu.make_async_remote_copy(
+            src_ref=maptile.at[frm], dst_ref=map_v.at[frm], send_sem=m_send.at[frm],
+            recv_sem=m_recv.at[frm], device_id=(frm, f), device_id_type=MESH,
         )
 
     own_block = pltpu.make_async_copy(child_v.at[d], arrived.at[d], local.at[0])
@@ -102,16 +102,23 @@
 
     def send_blocks():
         def step(k, _):
-            map_copy(k).start()
-            block_copy(k).start()
+            early = jnp.where(k < NS, lax.rem(d + k, NS), NS + lax.rem(d + k, NL - NS))
+            to = jnp.where(f == 0, early, lax.rem(d + k, NL))
+
+            @pl.when(to != d)
+            def _():
+                map_copy(to).start()
+                block_copy(to).start()
+
             return 0
 
-        lax.fori_loop(1, NL, step, 0)
+        lax.fori_loop(0, NL, step, 0)
 
     def receive_blocks():
         def step(k, _):
-            map_in(k).wait_recv()
-            block_in(k).wait_recv()
+            frm = lax.rem(d + k, NL)
+            map_in(frm).wait_recv()
+            block_in(frm).wait_recv()
             return 0
 
         lax.fori_loop(1, NL, step, 0)
@@ -175,32 +182,28 @@
     onward = f + 2 - 4 * core
     has_onward = ((core == 0) & (x < 3)) | ((core == 1) & (x > 1))
 
-    @pl.when(f != 0)
-    def _():
-        def passing(n, _):
-            j = 2 * n + core
-            chunk_copy(j, 0, 0).wait_recv()
-
-            @pl.when(f >= 2)
+    def pass_on(n):
+        j = 2 * n + core
+        chunk_copy(j, 0, 0).wait_recv()
+
+        @pl.when(f >= 2)
+        def _():
+            @pl.when(has_onward)
             def _():
-                @pl.when(has_onward)
-                def _():
-                    chunk_copy(j, onward, 0).start()
-
-                chunk_copy(j, pair, 1).start()
-
-            return 0
-
+                chunk_copy(j, onward, 0).start()
+
+            chunk_copy(j, pair, 1).start()
+
+        @pl.when((f == 1) & (n == 0))
+        def _():
+            send_blocks()
+
+    def take_rest():
         def ending(n, _):
             chunk_copy(2 * n + 1 - core, 0, 0).wait_recv()
             return 0
 
-        lax.fori_loop(0, NC // 2, passing, 0)
         lax.fori_loop(0, NC // 2, ending, 0)
-
-    @pl.when(f == 1)
-    def _():
-        send_blocks()
 
     def where_from(i, lead):
         r = 0 if lead else f * CB + i
@@ -232,12 +235,12 @@
         @pl.when(at_source)
         def _():
             mine = piece_of(held, r_at, y)
-            act(z_copy(mine, i, True))
-            act(z_copy(mine, i, False))
             for k in range(1, NY):
                 q = lax.rem(y + k, NY)
                 act(piece_copy(piece_of(held, r_at, q), i, q, z, q, qa_send.at[i, k]))
-            for k in range(1, NY):
+            act(z_copy(mine, i, True))
+            act(z_copy(mine, i, False))
+            for k in (1, NY - 1):
                 q = lax.rem(y + k, NY)
                 act(piece_copy(mine, i, y, z, q, qy_send.at[i, k]))
             if not lead:
@@ -259,14 +262,34 @@
             def _():
                 act(z_copy(mine, i, False))
 
-            for k in range(1, NY):
+            for k in (1, NY - 1):
                 q = lax.rem(y + k, NY)
 
                 @pl.when((zr != 0) | (q != ys))
                 def _():
                     act(piece_copy(mine, i, y, z, q, qy_send.at[i, k]))
 
-                act(None, i, q, late=True)
+    def relay_row(i, act, lead):
+        r_loc, ys, zr = where_from(i, lead)
+        held, r_at = (match, i) if lead else (rows, r_loc)
+        at_source = (zr == 0) & (y == ys)
+        back = jnp.where(i % 2 == 0, NY - 1, 1)
+        q, to = lax.rem(y + back, NY), lax.rem(y + NY - back, NY)
+
+        @pl.when(at_source)
+        def _():
+            act(piece_copy(piece_of(held, r_at, q), i, q, z, to, qy_send.at[i, 0]))
+
+        @pl.when(jnp.logical_not(at_source))
+        def _():
+            act(None, i, q)
+
+            @pl.when((zr != 0) | (to != ys))
+            def _():
+                act(piece_copy(piece_of(match, i, q), i, q, z, to, qy_send.at[i, 0]))
+
+            act(None, i, to, late=True)
+            act(None, i, lax.rem(y + 2, NY), late=True)
 
     def piece_in(i, q):
         piece_copy(piece_of(match, i, q), i, q, z, lax.rem(y + 1, NY), qy_send.at[i, 1]).wait_recv()
@@ -286,9 +309,9 @@
         else:
             copy.wait_send()
 
-    def run(act, first, last, lead):
+    def run(turn, act, first, last, lead):
         def step(i, _):
-            match_row(i, act, lead)
+            turn(i, act, lead)
             return 0
 
         lax.fori_loop(first, last, step, 0)
@@ -305,50 +328,91 @@
             recv_sem=t_recv.at[i - CB], device_id=(d, to), device_id_type=MESH,
         )
 
-    keep_rows = pltpu.make_async_copy(rows, rows_out, local.at[7])
-    keep_rows.start()
-    run(begin, 0, CB, False)
     is_root = (d == 0) & (f == 0)
     keep_pivots = pltpu.make_async_copy(pivots, pivots_out, local.at[6])
 
-    @pl.when(is_root)
-    def _():
-        work[...] = rows[0:W, :]
-        factor_lead(work, pivots, inv)
-        keep_pivots.start()
-        match[CB * B :, :] = jnp.zeros((LR * B, W), F32)
-        for i in range(PANELS):
-            for j in range(i + 1):
-                n = i * (i + 1) // 2 + j
-                at = (CB + n // PANELS) * B
-                to = n % PANELS * B
-                match[at : at + B, to : to + B] = inv[i * B : i * B + B, j * B : j * B + B]
-        for i in range(CB, NR):
-            lead_copy(i, 2, 0).start()
-            lead_copy(i, NF - 2, 1).start()
-
-    @pl.when((d == 0) & (core == 0) & (f != 0))
-    def _():
-        for i in range(CB, NR):
+    def lead_done(k):
+        match[pl.ds(pl.multiple_of((CB + k) * B, B), B), :] = inv[pl.ds(pl.multiple_of(k * B, B), B), :]
+        lead_copy(CB + k, 2, 0).start()
+        lead_copy(CB + k, NF - 2, 1).start()
+        match_row(CB + k, begin, True)
+        relay_row(CB + k, begin, True)
+
+    def pass_lead(i):
+        @pl.when((d == 0) & (f != 0))
+        def _():
             lead_copy(i, 0, 0).wait_recv()
 
             @pl.when(f == 2)
             def _():
                 lead_copy(i, 4, 0).start()
 
+        match_row(i, begin, True)
+
+    behind = jnp.where(f == 0, 0, jnp.where(d < NS, NC // 2, LAG))
+
+    def turn(n, _):
+        @pl.when((f != 0) & (n < NC // 2))
+        def _():
+            pass_on(n)
+
+        @pl.when((f != 0) & (d < NS) & (n == NC // 2))
+        def _():
+            take_rest()
+
+        m = n - behind
+
+        @pl.when((m >= 0) & (m < CB))
+        def _():
+            match_row(m, begin, False)
+
+        @pl.when((m >= RELAY_LAG) & (m < CB + RELAY_LAG))
+        def _():
+            relay_row(m - RELAY_LAG, begin, False)
+
+        i = m - jnp.where(d == 0, jnp.where(f >= 5, -LR, 0), LEAD_TURN) + CB
+        takes_lead = (core == 0) & jnp.logical_not(is_root)
+
+        @pl.when(takes_lead & (i >= CB) & (i < NR))
+        def _():
+            pass_lead(i)
+
+        @pl.when(takes_lead & (i >= CB + RELAY_LAG) & (i < NR + RELAY_LAG))
+        def _():
+            relay_row(i - RELAY_LAG, begin, True)
+
+        return 0
+
+    lax.fori_loop(0, NC // 2 + max(CB, LEAD_TURN + LR) + RELAY_LAG, turn, 0)
+
+    @pl.when(is_root)
+    def _():
+        work[...] = rows[0:W, :]
+        factor_lead(work, pivots, inv, lead_done)
+        keep_pivots.start()
+
+    @pl.when((f != 0) & (d >= NS))
+    def _():
+        take_rest()
+
+    keep_rows = pltpu.make_async_copy(rows, rows_out, local.at[7])
+    keep_rows.start()
+
+    @pl.when(f != 0)
+    def _():
+        receive_blocks()
+
+    run(match_row, finish, 0, CB, False)
+    run(relay_row, finish, 0, CB, False)
+    keep_match = pltpu.make_async_copy(
+        match.at[pl.ds(0, CB * B)], match_out.at[pl.ds(0, CB * B)], local.at[5]
+    )
+    keep_match.start()
+
     @pl.when(core == 0)
     def _():
-        run(begin, CB, NR, True)
-
-    @pl.when(f != 0)
-    def _():
-        receive_blocks()
-
-    run(finish, 0, CB, False)
-
-    @pl.when(core == 0)
-    def _():
-        run(finish, CB, NR, True)
+        run(match_row, finish, CB, NR, True)
+        run(relay_row, finish, CB, NR, True)
         for i in range(CB, NR):
             twin_copy(i, f + 1).start()
         for i in range(CB, NR):
@@ -359,8 +423,10 @@
         for i in range(CB, NR):
             twin_copy(i, f - 1).wait_recv()
 
-    keep_match = pltpu.make_async_copy(match, match_out, local.at[5])
-    keep_match.start()
+    keep_lead = pltpu.make_async_copy(
+        match.at[pl.ds(CB * B, LR * B)], match_out.at[pl.ds(CB * B, LR * B)], local.at[8]
+    )
+    keep_lead.start()
 
     @pl.when(is_root)
     def _():
@@ -375,8 +441,9 @@
             lead_copy(i, 4, 0).wait_send()
 
     def sent(k, _):
-        map_copy(k).wait_send()
-        block_copy(k).wait_send()
+        to = lax.rem(d + k, NL)
+        map_copy(to).wait_send()
+        block_copy(to).wait_send()
         return 0
 
     lax.fori_loop(1, NL, sent, 0)
@@ -406,6 +473,7 @@
 
     keep_rows.wait()
     keep_match.wait()
+    keep_lead.wait()
     pltpu.make_async_copy(code_v, code, local.at[2]).wait()
     pltpu.make_async_copy(arrived, arrived_out, local.at[0]).wait()
 
@@ -483,7 +551,7 @@
 NN = ((1,), (0,))
 
 
-def factor_lead(work, pivots, inv):
+def factor_lead(work, pivots, inv, done):
     r = lax.broadcasted_iota(jnp.int32, (B, B), 0)
     c = lax.broadcasted_iota(jnp.int32, (B, B), 1)
     row_block = lax.broadcasted_iota(jnp.int32, (W, B), 0) // B
@@ -499,6 +567,7 @@
         before = jnp.where(col_block < k, work[at, :], 0.0)
         inv[at, :] = -dot_exact(inverse, dot_exact(before, inv[...], NN), NN)
         inv[at, at] = inverse
+        done(k)
         work[...] = work[...] - dot_exact(lower, lower, NT)
         work[:, at] = lower
         return 0
@@ -532,14 +601,7 @@
 
     @pl.when(n == 0)
     def _():
-        inv_h[...] = jnp.zeros_like(inv_h)
-        inv_l[...] = jnp.zeros_like(inv_l)
-        for i in range(PANELS):
-            for j in range(i + 1):
-                k = i * (i + 1) // 2 + j
-                ks, ls = (CB + k // PANELS) * B, k % PANELS * B
-                at, to = slice(i * B, i * B + B), slice(j * B, j * B + B)
-                inv_h[at, to], inv_l[at, to] = halves(match[ks : ks + B, ls : ls + B])
+        inv_h[...], inv_l[...] = halves(match[CB * B :, :])
         for i in range(0, CB, STEP):
             at = slice(i * B, (i + STEP) * B)
             lower = dot_split(halves(match[at, :]), (inv_h[...], inv_l[...]))

time: 159 us -> 151 us (0.950)
  the two profiles are of different devices: /device:TPU:133 before, /device:TPU:167 now
where the time goes in v3:
time: 151 us; the launch traced here: 148 us
  Pallas kernels  145 us (96%)
  local copies, waits for them, and re-layouts  2.77 us (2%)
    pallas_call x1, Pallas kernels, exchange_call(): pl.pallas_call(exchange, out_shape=(shape((NL, B, B), F32), shape((8, B),...  130 us
    pallas_call x1, Pallas kernels, finish_call(): pl.pallas_call(finish_kernel, out_shape=jax.ShapeDtypeStruct(front.shape,...  15.2 us

profile of v3, /device:TPU:167, one launch (start us, length us, event | category | flops | bytes accessed | tf_op | source)
XLA Modules:
  0.0 148.2 jit_solution(14928974761893801075)
XLA Ops:
  0.0 1.4 copy.5.pattern
  1.4 1.4 broadcast_in_dim.8.maptile
  2.8 130.2 %shard_map.46 = (f32[32,128,128]{2,1,0:T(8,128)}, s32[8,128]{1,0:T(8,128)}, f32[1280,512]{1,0:T(8,128)}, f32[1536,512]{1,0:T(8,128)}, f32[4,128,128]{2,1,0:T(8,128)}) custom-call(f32[32,128,128]{2,1,0:T(8,128)} %bitcast.2, s32[32,8,128]{2,1,0:T(8,128)} %broadcast_in_dim.8.maptile, f32[1280,1024]{1,0:T(8,128)} %front.3, s32[10,8]{1,0:T(8,128)} %copy.5.pattern), custom_call_target="tpu_custom_call" | custom-call | tf_op jit(solution)/shard_map/pallas_call | solution.py:484
  133.0 15.2 %shard_map.47 = f32[1280,1024]{1,0:T(8,128)} custom-call(s32[8,128]{1,0:T(8,128)} %get-tuple-element.10.code, s32[10,8]{1,0:T(8,128)} %copy.5.pattern, f32[1280,1024]{1,0:T(8,128)} %front.3, f32[1280,512]{1,0:T(8,128)} %get-tuple-element.11.rows, f32[1536,512]{1,0:T(8,128)} %get-tuple-element.12.match, f32[4,128,128]{2,1,0:T(8,128)} %get-tuple-element.13.pivots, ...), custom_call_target="tpu_custom_call" | custom-call | tf_op jit(solution)/shard_map/pallas_call | solution.py:639

commit v4 on v3

--- a/solution.py
+++ b/solution.py
@@ -370,7 +370,8 @@
         def _():
             relay_row(m - RELAY_LAG, begin, False)
 
-        i = m - jnp.where(d == 0, jnp.where(f >= 5, -LR, 0), LEAD_TURN) + CB
+        late = jnp.where(d == 0, 0, LEAD_TURN)
+        i = m - jnp.where((f >= 5) & (d < NY), -LR, late) + CB
         takes_lead = (core == 0) & jnp.logical_not(is_root)
 
         @pl.when(takes_lead & (i >= CB) & (i < NR))
@@ -411,10 +412,13 @@
 
     @pl.when(core == 0)
     def _():
-        run(match_row, finish, CB, NR, True)
-        run(relay_row, finish, CB, NR, True)
-        for i in range(CB, NR):
+        def hand_over(i, _):
+            match_row(i, finish, True)
+            relay_row(i, finish, True)
             twin_copy(i, f + 1).start()
+            return 0
+
+        lax.fori_loop(CB, NR, hand_over, 0)
         for i in range(CB, NR):
             twin_copy(i, f + 1).wait_send()
 

time: 151 us -> 147 us (0.974); the launches traced: 148 us -> 147 us
  no operation moved by 1% of the time
where the time goes in v4:
time: 147 us
  Pallas kernels  144 us (98%)
  local copies, waits for them, and re-layouts  2.77 us (2%)
    pallas_call x1, Pallas kernels, exchange_call(): pl.pallas_call(exchange, out_shape=(shape((NL, B, B), F32), shape((8, B),...  129 us
    pallas_call x1, Pallas kernels, finish_call(): pl.pallas_call(finish_kernel, out_shape=jax.ShapeDtypeStruct(front.shape,...  15.2 us

profile of v4, /device:TPU:167, one launch (start us, length us, event | category | flops | bytes accessed | tf_op | source)
XLA Modules:
  0.0 147.1 jit_solution(16024369010413744118)
XLA Ops:
  0.0 1.4 copy.5.pattern
  1.4 1.4 broadcast_in_dim.8.maptile
  2.8 129.1 %shard_map.46 = (f32[32,128,128]{2,1,0:T(8,128)}, s32[8,128]{1,0:T(8,128)}, f32[1280,512]{1,0:T(8,128)}, f32[1536,512]{1,0:T(8,128)}, f32[4,128,128]{2,1,0:T(8,128)}) custom-call(f32[32,128,128]{2,1,0:T(8,128)} %bitcast.2, s32[32,8,128]{2,1,0:T(8,128)} %broadcast_in_dim.8.maptile, f32[1280,1024]{1,0:T(8,128)} %front.3, s32[10,8]{1,0:T(8,128)} %copy.5.pattern), custom_call_target="tpu_custom_call" | custom-call | tf_op jit(solution)/shard_map/pallas_call | solution.py:488
  131.9 15.2 %shard_map.47 = f32[1280,1024]{1,0:T(8,128)} custom-call(s32[8,128]{1,0:T(8,128)} %get-tuple-element.10.code, s32[10,8]{1,0:T(8,128)} %copy.5.pattern, f32[1280,1024]{1,0:T(8,128)} %front.3, f32[1280,512]{1,0:T(8,128)} %get-tuple-element.11.rows, f32[1536,512]{1,0:T(8,128)} %get-tuple-element.12.match, f32[4,128,128]{2,1,0:T(8,128)} %get-tuple-element.13.pivots, ...), custom_call_target="tpu_custom_call" | custom-call | tf_op jit(solution)/shard_map/pallas_call | solution.py:643

commit v5 on v4

--- a/solution.py
+++ b/solution.py
@@ -592,6 +592,14 @@
     return dot(ah, bh) + (dot(al, bh) + dot(ah, bl))
 
 
+def solve(a, inv_h, inv_l):
+    high, low = halves(a)
+    n = W // 2
+    left = dot_split((high[:, :n], low[:, :n]), (inv_h[:n, :n], inv_l[:n, :n]))
+    right = dot_split((high, low), (inv_h[n:, :], inv_l[n:, :]))
+    return jnp.concatenate([left, right], axis=1)
+
+
 STEP = 2
 
 
@@ -608,10 +616,10 @@
         inv_h[...], inv_l[...] = halves(match[CB * B :, :])
         for i in range(0, CB, STEP):
             at = slice(i * B, (i + STEP) * B)
-            lower = dot_split(halves(match[at, :]), (inv_h[...], inv_l[...]))
+            lower = solve(match[at, :], inv_h, inv_l)
             across_h[at, :], across_l[at, :] = halves(lower)
 
-    lower = dot_split(halves(rows[...]), (inv_h[...], inv_l[...]))
+    lower = solve(rows[...], inv_h, inv_l)
     product = dot_split(halves(lower), (across_h[...], across_l[...]))
     for rr in range(STEP):
         r = n * STEP + rr

time: 147 us -> 149 us (1.014)
  Pallas kernels: 144 us -> 146 us
    pallas_call x1, Pallas kernels: 15.2 us -> 17 us  [finish_call(): pl.pallas_call(finish_kernel, out_shape=jax.ShapeDtypeStruct(front.shape,...]
where the time goes in v5:
time: 149 us
  Pallas kernels  146 us (98%)
  local copies, waits for them, and re-layouts  2.77 us (2%)
    pallas_call x1, Pallas kernels, exchange_call(): pl.pallas_call(exchange, out_shape=(shape((NL, B, B), F32), shape((8, B),...  129 us
    pallas_call x1, Pallas kernels, finish_call(): pl.pallas_call(finish_kernel, out_shape=jax.ShapeDtypeStruct(front.shape,...  17 us

profile of v5, /device:TPU:167, one launch (start us, length us, event | category | flops | bytes accessed | tf_op | source)
XLA Modules:
  0.0 148.8 jit_solution(13731440726455148806)
XLA Ops:
  0.0 1.4 copy.5.pattern
  1.4 1.4 broadcast_in_dim.8.maptile
  2.8 129.1 %shard_map.46 = (f32[32,128,128]{2,1,0:T(8,128)}, s32[8,128]{1,0:T(8,128)}, f32[1280,512]{1,0:T(8,128)}, f32[1536,512]{1,0:T(8,128)}, f32[4,128,128]{2,1,0:T(8,128)}) custom-call(f32[32,128,128]{2,1,0:T(8,128)} %bitcast.2, s32[32,8,128]{2,1,0:T(8,128)} %broadcast_in_dim.8.maptile, f32[1280,1024]{1,0:T(8,128)} %front.3, s32[10,8]{1,0:T(8,128)} %copy.5.pattern), custom_call_target="tpu_custom_call" | custom-call | tf_op jit(solution)/shard_map/pallas_call | solution.py:488
  131.9 17.0 %shard_map.47 = f32[1280,1024]{1,0:T(8,128)} custom-call(s32[8,128]{1,0:T(8,128)} %get-tuple-element.10.code, s32[10,8]{1,0:T(8,128)} %copy.5.pattern, f32[1280,1024]{1,0:T(8,128)} %front.3, f32[1280,512]{1,0:T(8,128)} %get-tuple-element.11.rows, f32[1536,512]{1,0:T(8,128)} %get-tuple-element.12.match, f32[4,128,128]{2,1,0:T(8,128)} %get-tuple-element.13.pivots, ...), custom_call_target="tpu_custom_call" | custom-call | tf_op jit(solution)/shard_map/pallas_call | solution.py:651
